TPU v7x, 256 devices: a whole 4x4x8 slice. The times are simulated.
256 devices in a mesh: grp: 4 (over z_hi), gx: 32 (over x, z_lo, y), gy: 2 (over core).
Axes of the slice: x: 4, y: 4, z: 8 (z_hi: 4, z_lo: 2; z = z_hi * 2 + z_lo), core: 2. Of those that a mesh axis runs over, the one named last changes fastest.
Arguments:
- fluid_temp: float32 [512, 256, 1024], P('gx', 'gy', 'grp'), may hold values from -6 to 6
- active: int32 [512, 256, 1024], P('gx', 'gy', 'grp'), may hold values 0 or 1
- fin_temp: float32 [256, 1024, 512], P('grp', 'gx', 'gy'), may hold values from -6 to 6
- fin_source: float32 [256, 1024, 512], P('grp', 'gx', 'gy'), may hold values from -6 to 6
- wall_owner: int32 [32, 2, 2048, 1], P('gx', 'gy'), may hold values from 0 to 31, as said below
- wall_target: int32 [32, 2, 2048], P('gx', 'gy'), may hold values from 0 to 8191, as said below
Outputs:
- fluid_new: float32 [512, 256, 1024], P('gx', 'gy', 'grp')
- fin_new: float32 [256, 1024, 512], P('grp', 'gx', 'gy')
Inputs may be any that keep to these rules, and one draw needn't show every extreme that they name: `wall_owner`: among the 2048 wall cells of one column block (a, b), exactly 128 name the owner a and at most 128 name any one owner; in every draw one owner is named by exactly 128 wall cells of every column block. `wall_target`: wall cell w = i * 128 + j names a root cell (2 * i + di) * 256 + 2 * j + dj of the 2 x 2 patch beneath it, di and dj being 0 or 1; the first wall cell of a block names its patch's first root cell, the last one its patch's last.
All inputs are finite; a program needn't handle non-finite values. No bound on the sum of `active` on one device may be relied on, other than what follows from the above.
Results may differ from a plain program's by a relative error of at most 0.00002.
Values sent between devices are 32-bit elements; how exact they have to be, the bound alone decides.
A program may use at most 64 MiB of HBM per device.

v0:
```python
import jax
import jax.numpy as jnp
from jax import lax
from jax.sharding import PartitionSpec as P

FLUID_DIFFUSION = 1.0
FIN_CONDUCTION = 1.0
HEAT_COEF = 1.0


def padded_2(block, sides, width):
    for axis, dim in sides:
        count = lax.axis_size(axis)
        forward = [(i, i + 1) for i in range(count - 1)]
        backward = [(target, source) for source, target in forward]
        low = lax.ppermute(
            lax.slice_in_dim(block, block.shape[dim] - width, None, axis=dim), axis, forward
        )
        high = lax.ppermute(lax.slice_in_dim(block, 0, width, axis=dim), axis, backward)
        block = jnp.concatenate([low, block, high], axis=dim)
    return block


def six_sum(padded):
    return (
        padded[2:, 1:-1, 1:-1]
        + padded[:-2, 1:-1, 1:-1]
        + padded[1:-1, 2:, 1:-1]
        + padded[1:-1, :-2, 1:-1]
        + padded[1:-1, 1:-1, 2:]
        + padded[1:-1, 1:-1, :-2]
    )


def fin_from_padded(padded, field):
    return (1.0 + 6.0 * FIN_CONDUCTION) * field - FIN_CONDUCTION * six_sum(padded)


def fin_image(field):
    padded = padded_2(field, (("grp", 0), ("gx", 1), ("gy", 2)), 1)
    return fin_from_padded(padded, field)


def fluid_padded_apart(field):
    return padded_2(field, (("grp", 2), ("gx", 0), ("gy", 1)), 1)


def fluid_update(padded, field, fluid_temp, update_mask, ghost, on_wall):
    lowest = lax.broadcasted_iota(jnp.int32, field.shape, 2) == 0
    below = jnp.where(lowest & on_wall, ghost[:, :, None], 0.0)
    neighbours = six_sum(padded) + below
    updated = (fluid_temp + FLUID_DIFFUSION * neighbours) / (1.0 + 6.0 * FLUID_DIFFUSION)
    return jnp.where(update_mask, updated, field)


def local(fluid_temp, active, fin_temp, fin_source, wall_owner, wall_target):
    first_cells, second_cells, third_cells = fluid_temp.shape
    fin_depth, fin_width, fin_height = fin_temp.shape
    owner_count = lax.axis_size("gx")
    wall_cells = first_cells * second_cells
    capacity = min(wall_cells, max(2, 2 * wall_cells // owner_count))
    on_wall = lax.axis_index("grp") == 0
    owners = wall_owner[0, 0, :, 0]
    targets = wall_target[0, 0, :]
    onehot = (owners[:, None] == jnp.arange(owner_count, dtype=jnp.int32)[None, :]).astype(
        jnp.int32
    )
    ranks = jnp.sum((jnp.cumsum(onehot, axis=0) - onehot) * onehot, axis=1)
    slot_index = owners * capacity + ranks
    wall_temps = fluid_temp[:, :, 0].reshape(-1)
    send_temps = jnp.zeros((owner_count * capacity,), jnp.float32).at[slot_index].set(wall_temps)
    send_targets = (
        jnp.full((owner_count * capacity,), -1.0, jnp.float32)
        .at[slot_index]
        .set(targets.astype(jnp.float32))
    )
    received = lax.all_to_all(
        jnp.stack([send_temps, send_targets]), "gx", split_axis=1, concat_axis=1, tiled=True
    )
    got_targets = received[1].astype(jnp.int32)
    valid = (got_targets >= 0) & on_wall
    safe_targets = jnp.where(valid, got_targets, 0)
    surface = fin_temp[0].reshape(-1)
    fin_wall = jnp.where(valid, surface[safe_targets], 0.0)
    heat_flux = jnp.where(valid, HEAT_COEF * (received[0] - fin_wall), 0.0)
    deposit = jax.ops.segment_sum(heat_flux, safe_targets, num_segments=fin_width * fin_height)
    returned = lax.all_to_all(fin_wall, "gx", split_axis=0, concat_axis=0, tiled=True)
    ghost = returned[slot_index].reshape(first_cells, second_cells)
    fin_rhs = fin_temp + fin_source
    fin_rhs = fin_rhs.at[0].add(deposit.reshape(fin_width, fin_height))
    diag = 1.0 + 6.0 * FIN_CONDUCTION
    spectral = 6.0 * FIN_CONDUCTION / diag
    omega = 1.0 / (1.0 - spectral * spectral / 2.0)
    shape = fluid_temp.shape
    colour = (
        lax.broadcasted_iota(jnp.int32, shape, 0)
        + lax.broadcasted_iota(jnp.int32, shape, 1)
        + lax.broadcasted_iota(jnp.int32, shape, 2)
    ) % 2
    red_mask = (colour == 0) & (active == 1)
    black_mask = (colour == 1) & (active == 1)
    first_state = fin_temp + (fin_rhs - fin_image(fin_temp)) / diag
    second_image = fin_image(first_state)
    red_temp = fluid_update(
        fluid_padded_apart(fluid_temp), fluid_temp, fluid_temp, red_mask, ghost, on_wall
    )
    fluid_new = fluid_update(
        fluid_padded_apart(red_temp), red_temp, fluid_temp, black_mask, ghost, on_wall
    )
    fin_new = omega * (first_state + (fin_rhs - second_image) / diag - fin_temp) + fin_temp
    return (fluid_new, fin_new)


def solution(mesh):
    in_specs = (
        P("gx", "gy", "grp"),
        P("gx", "gy", "grp"),
        P("grp", "gx", "gy"),
        P("grp", "gx", "gy"),
        P("gx", "gy", None, None),
        P("gx", "gy", None),
    )
    out_specs = (P("gx", "gy", "grp"), P("grp", "gx", "gy"))
    return jax.shard_map(local, mesh=mesh, in_specs=in_specs, out_specs=out_specs, check_vma=False)
```

profile of v0, /device:TPU:120, one launch (start us, length us, event | category | flops | bytes accessed | tf_op | source)
XLA Modules:
  0.0 321.8 jit_solution(9975414038074076085)
XLA Ops:
  4.9 9.1 %reduce-window.6 = s32[32,16,128]{2,1,0:T(8,128)S(1)} reduce-window(s32[32,16,128]{2,1,0:T(8,128)S(1)} %fusion.41, s32[]{:T(128)} %constant.65.clone.1), window={size=1x1x128 pad=0_0x0_0x127_0}, to_apply=%region_0.0 | reduce-window | flops 8323072 | bytes 524292 | tf_op jit(solution)/shard_map/reduce-window
  14.8 8.1 %scatter_custom_fusion = f32[4096]{0:T(1024)S(1)} fusion(s32[2048]{0:T(1024)S(1)} %bitcast.84, f32[2048]{0:T(1024)S(1)} %bitcast.88, f32[]{:T(128)} %constant.70.clone.1), kind=kCustom, calls=%fused_computation.160 | custom fusion | bytes 16388 | tf_op jit(solution)/shard_map/scatter | solution.py:71
  22.9 8.1 %scatter_custom_fusion.1 = f32[4096]{0:T(1024)S(1)} fusion(s32[2048]{0:T(1024)S(1)} %bitcast.85, f32[2048]{0:T(1024)S(1)} %bitcast.89, f32[]{:T(128)} %constant.73.clone.1), kind=kCustom, calls=%fused_computation.158 | custom fusion | bytes 16388 | tf_op jit(solution)/shard_map/scatter | solution.py:75
  31.6 8.2 %all-to-all-start = ((f32[2,32,128]{2,0,1:T(2,128)}), f32[2,32,128]{2,0,1:T(2,128)S(1)}, u32[]{:S(2)}, u32[]{:S(2)}) async-start(f32[2,32,128]{2,0,1:T(2,128)} %pad_maximum_fusion.88), calls=%async_computation | async-start | bytes 65536 | tf_op jit(solution)/shard_map/all_to_all | solution.py:77
  39.8 5.9 %copy_add_fusion = (f32[64,32,256]{2,0,1:T(8,128)}, f32[64,32,256]{2,0,1:T(8,128)S(1)}) fusion(f32[64,32,256]{2,1,0:T(8,128)} %param.11, f32[64,32,256]{2,1,0:T(8,128)} %param.10), kind=kLoop, calls=%fused_computation.124 | loop fusion | flops 524288 | bytes 8388608 | tf_op jit(solution)/shard_map/add | solution.py:89
  47.7 6.0 %collective-permute-start.13 = (f32[1,32,256]{2,0,1:T(1,128)S(1)}, f32[1,32,256]{2,0,1:T(1,128)S(1)}, u32[]{:S(2)}, u32[]{:S(2)}) collective-permute-start(f32[1,32,256]{2,0,1:T(1,128)S(1)} %copy.116), channel_id=1, source_target_pairs={{0,64},{64,128},{128,192},{1,65},{65,129},{129,193},{2,66},{66,130... | collective-permute-start | bytes 98312 | tf_op jit(solution)/shard_map/ppermute | solution.py:16
  54.1 4.8 %collective-permute-start = (f32[16,128,1]{1,0,2:T(8,128)S(1)}, f32[16,128,1]{1,0,2:T(8,128)S(1)}, u32[]{:S(2)}, u32[]{:S(2)}) collective-permute-start(f32[16,128,1]{1,0,2:T(8,128)S(1)} %copy.133), channel_id=1, source_target_pairs={{0,64},{64,128},{128,192},{1,65},{65,129},{129,193},{2,66},{66,130... | collective-permute-start | bytes 24584 | tf_op jit(solution)/shard_map/ppermute | solution.py:16
  68.0 6.1 %collective-permute-start.3 = (f32[1,128,258]{1,2,0:T(8,128)}, f32[1,128,258]{1,2,0:T(8,128)}, u32[]{:S(2)}, u32[]{:S(2)}) collective-permute-start(f32[1,128,258]{1,2,0:T(8,128)} %get-tuple-element.40), channel_id=1, source_target_pairs={{0,2},{2,4},{4,6},{6,8},{8,10},{10,12},{12,14},{14,16},{16,18},{18... | collective-permute-start | bytes 396296 | tf_op jit(solution)/shard_map/ppermute | solution.py:16
  76.1 6.9 %collective-permute-start.15 = (f32[66,1,256]{2,0,1:T(8,128)S(1)}, f32[66,1,256]{2,0,1:T(8,128)S(1)}, u32[]{:S(2)}, u32[]{:S(2)}) collective-permute-start(f32[66,1,256]{2,0,1:T(8,128)S(1)} %get-tuple-element.36), channel_id=1, source_target_pairs={{0,2},{2,4},{4,6},{6,8},{8,10},{10,12},{12,14},{14,16},{16,18},{18... | collective-permute-start | bytes 202760 | tf_op jit(solution)/shard_map/ppermute | solution.py:16
  83.1 23.0 %gather_fusion = f32[4096]{0:T(1024)S(1)} fusion(f32[8192]{0:T(1024)S(1)} %bitcast.54, s32[4096]{0:T(1024)S(1)} %broadcast_clamp_fusion), kind=kCustom, calls=%fused_computation | custom fusion | bytes 49152 | tf_op jit(solution)/shard_map/gather | solution.py:84
  106.8 8.0 %all-to-all-start.1 = ((f32[32,128,1]{1,2,0:T(1,128)}), f32[32,128,1]{1,2,0:T(1,128)S(1)}, u32[]{:S(2)}, u32[]{:S(2)}) async-start(f32[32,128,1]{1,2,0:T(1,128)} %bitcast.19), calls=%async_computation.1 | async-start | bytes 32768 | tf_op jit(solution)/shard_map/all_to_all | solution.py:87
  114.8 29.4 %scatter_custom_fusion.2 = f32[8192]{0:T(1024)} fusion(s32[4096]{0:T(1024)S(1)} %bitcast.87, f32[4096]{0:T(1024)S(1)} %get-tuple-element.20, f32[]{:T(128)} %constant.70.clone.1), kind=kCustom, calls=%fused_computation.153 | custom fusion | flops 4096 | bytes 32772 | tf_op jit(solution)/shard_map/scatter-add | solution.py:86
  153.6 4.2 %collective-permute-start.17 = (f32[66,34,1]{0,1,2:T(8,128)}, f32[66,34,1]{0,1,2:T(8,128)}, u32[]{:S(2)}, u32[]{:S(2)}) collective-permute-start(f32[66,34,1]{0,1,2:T(8,128)} %copy.121), channel_id=1, source_target_pairs={{0,1},{2,3},{4,5},{6,7},{8,9},{10,11},{12,13},{14,15},{16,17},{18,... | collective-permute-start | bytes 26936 | tf_op jit(solution)/shard_map/ppermute | solution.py:16
  160.6 11.9 %gather_fusion.1 = f32[2048]{0:T(1024)S(1)} fusion(f32[4096]{0:T(1024)S(1)} %bitcast.55, s32[2048]{0:T(1024)} %broadcast_clamp_fusion.1), kind=kCustom, calls=%fused_computation.1 | custom fusion | bytes 24576 | tf_op jit(solution)/shard_map/gather | solution.py:88
  176.0 13.9 %fusion.23 = f32[64,32,256]{2,0,1:T(8,128)} fusion(f32[64,32,256]{2,0,1:T(8,128)} %copy-done.1, f32[64,32,256]{2,0,1:T(8,128)} %scatter-add.13, f32[66,34,1]{2,0,1:T(8,128)} %copy.122, f32[66,1,256]{2,0,1:T(8,128)} %copy-done.7, f32[66,1,256]{2,0,1:T(8,128)} %copy-done.8, f32[1,32,256]{2,0,1:T(1,128)S(1)} %collective-permute-done.12, ...), kind=kLoop, calls=%fused_computation.56 | loop fusion | flops 14680064 | bytes 6510112 | tf_op jit(solution)/shard_map/add | solution.py:102
  207.4 6.0 %collective-permute-start.19 = (f32[1,32,256]{2,0,1:T(1,128)S(1)}, f32[1,32,256]{2,0,1:T(1,128)S(1)}, u32[]{:S(2)}, u32[]{:S(2)}) collective-permute-start(f32[1,32,256]{2,0,1:T(1,128)S(1)} %get-tuple-element.42), channel_id=1, source_target_pairs={{0,64},{64,128},{128,192},{1,65},{65,129},{129,193},{2,66},{66,130... | collective-permute-start | bytes 98312 | tf_op jit(solution)/shard_map/ppermute | solution.py:16
  218.0 8.2 %fusion.2 = (f32[16,128,256]{1,2,0:T(8,128)S(1)}, pred[16,128,256]{1,2,0:T(8,128)(4,1)}) fusion(f32[16,128,256]{1,2,0:T(8,128)S(1)} %copy.111, f32[16,128,1]{1,2,0:T(1,128)S(1)} %bitcast.65, f32[16,128,1]{1,2,0:T(1,128)S(1)} %bitcast.62, f32[18,1,258]{1,2,0:T(8,128)} %copy.89, f32[1,128,258]{1,2,0:T(8,128)S(1)} %collective-permute-done.2, ...), kind=kLoop, calls=%fused_computation.16 | loop fusion | flops 23068672 | bytes 7141920 | tf_op jit(solution)/shard_map/jit(_where)/select_n | solution.py:53
  228.2 4.8 %collective-permute-start.7 = (f32[16,128,1]{1,0,2:T(8,128)S(1)}, f32[16,128,1]{1,0,2:T(8,128)S(1)}, u32[]{:S(2)}, u32[]{:S(2)}) collective-permute-start(f32[16,128,1]{1,0,2:T(8,128)S(1)} %bitcast.90), channel_id=1, source_target_pairs={{64,0},{128,64},{192,128},{65,1},{129,65},{193,129},{66,2},{130,66... | collective-permute-start | bytes 24584 | tf_op jit(solution)/shard_map/ppermute | solution.py:19
  235.8 6.1 %collective-permute-start.21 = (f32[66,1,256]{2,0,1:T(8,128)S(1)}, f32[66,1,256]{2,0,1:T(8,128)S(1)}, u32[]{:S(2)}, u32[]{:S(2)}) collective-permute-start(f32[66,1,256]{2,0,1:T(8,128)S(1)} %get-tuple-element.34), channel_id=1, source_target_pairs={{0,2},{2,4},{4,6},{6,8},{8,10},{10,12},{12,14},{14,16},{16,18},{18... | collective-permute-start | bytes 202760 | tf_op jit(solution)/shard_map/ppermute | solution.py:16
  244.6 6.9 %collective-permute-start.9 = (f32[1,128,258]{1,2,0:T(8,128)}, f32[1,128,258]{1,2,0:T(8,128)}, u32[]{:S(2)}, u32[]{:S(2)}) collective-permute-start(f32[1,128,258]{1,2,0:T(8,128)} %get-tuple-element.38), channel_id=1, source_target_pairs={{0,2},{2,4},{4,6},{6,8},{8,10},{10,12},{12,14},{14,16},{16,18},{18... | collective-permute-start | bytes 396296 | tf_op jit(solution)/shard_map/ppermute | solution.py:16
  258.9 4.2 %collective-permute-start.23 = (f32[66,34,1]{0,1,2:T(8,128)}, f32[66,34,1]{0,1,2:T(8,128)}, u32[]{:S(2)}, u32[]{:S(2)}) collective-permute-start(f32[66,34,1]{0,1,2:T(8,128)} %copy.126), channel_id=1, source_target_pairs={{0,1},{2,3},{4,5},{6,7},{8,9},{10,11},{12,13},{14,15},{16,17},{18,... | collective-permute-start | bytes 26936 | tf_op jit(solution)/shard_map/ppermute | solution.py:16
  280.1 4.2 %collective-permute-start.11 = (f32[18,1,258]{2,0,1:T(8,128)}, f32[18,1,258]{2,0,1:T(8,128)}, u32[]{:S(2)}, u32[]{:S(2)}) collective-permute-start(f32[18,1,258]{2,0,1:T(8,128)} %copy.107), channel_id=1, source_target_pairs={{0,1},{2,3},{4,5},{6,7},{8,9},{10,11},{12,13},{14,15},{16,17},{18,... | collective-permute-start | bytes 55736 | tf_op jit(solution)/shard_map/ppermute | solution.py:16
  284.4 14.3 %fusion.14 = f32[64,32,256]{2,0,1:T(8,128)S(1)} fusion(f32[64,32,256]{2,0,1:T(8,128)} %fusion.23, f32[64,32,256]{2,0,1:T(8,128)} %scatter-add.13, f32[66,34,1]{2,0,1:T(8,128)} %copy.127, f32[66,1,256]{2,0,1:T(8,128)} %copy-done.9, f32[66,1,256]{2,0,1:T(8,128)} %copy-done.10, f32[1,32,256]{2,0,1:T(1,128)S(1)} %collective-permute-done.18, ...), kind=kLoop, calls=%fused_computation.29 | loop fusion | flops 16252928 | bytes 8607264 | tf_op jit(solution)/shard_map/add | solution.py:110
  307.4 11.5 %fusion.5 = f32[16,128,256]{1,2,0:T(8,128)} fusion(f32[16,128,256]{1,2,0:T(8,128)} %copy-done.3, f32[16,128,256]{1,2,0:T(8,128)S(1)} %copy.111, f32[16,128,1]{1,2,0:T(1,128)S(1)} %bitcast.68, f32[16,128,1]{1,2,0:T(1,128)S(1)} %bitcast.71, f32[18,1,258]{1,2,0:T(8,128)} %copy.108, f32[1,128,258]{1,2,0:T(8,128)S(1)} %collective-permute-done.8, ...), kind=kLoop, calls=%fused_computation.19 | loop fusion | flops 22544384 | bytes 7141920 | tf_op jit(solution)/shard_map/jit(_where)/select_n | solution.py:53
  (133 shorter events, 100.5 us)
Async XLA Ops:
  2.9 61.5 %collective-permute-start.1 = (f32[16,128,1]{1,0,2:T(8,128)S(1)}, f32[16,128,1]{1,0,2:T(8,128)S(1)}, u32[]{:S(2)}, u32[]{:S(2)}) collective-permute-start(f32[16,128,1]{1,0,2:T(8,128)S(1)} %copy.134), channel_id=1, source_target_pairs={{64,0},{128,64},{192,128},{65,1},{129,65},{193,129},{66,2},{130,66... | collective-permute-start | bytes 24584 | tf_op jit(solution)/shard_map/ppermute | solution.py:19
  31.6 51.4 %all-to-all-start = ((f32[2,32,128]{2,0,1:T(2,128)}), f32[2,32,128]{2,0,1:T(2,128)S(1)}, u32[]{:S(2)}, u32[]{:S(2)}) async-start(f32[2,32,128]{2,0,1:T(2,128)} %pad_maximum_fusion.88), calls=%async_computation | async-start | bytes 65536 | tf_op jit(solution)/shard_map/all_to_all | solution.py:77
  45.8 28.3 %collective-permute-start.12 = (f32[1,32,256]{2,0,1:T(1,128)S(1)}, f32[1,32,256]{2,0,1:T(1,128)S(1)}, u32[]{:S(2)}, u32[]{:S(2)}) collective-permute-start(f32[1,32,256]{2,0,1:T(1,128)S(1)} %slice.268), channel_id=1, source_target_pairs={{64,0},{128,64},{192,128},{65,1},{129,65},{193,129},{66,2},{130,66... | collective-permute-start | bytes 98312 | tf_op jit(solution)/shard_map/ppermute | solution.py:19
  47.7 26.3 %collective-permute-start.13 = (f32[1,32,256]{2,0,1:T(1,128)S(1)}, f32[1,32,256]{2,0,1:T(1,128)S(1)}, u32[]{:S(2)}, u32[]{:S(2)}) collective-permute-start(f32[1,32,256]{2,0,1:T(1,128)S(1)} %copy.116), channel_id=1, source_target_pairs={{0,64},{64,128},{128,192},{1,65},{65,129},{129,193},{2,66},{66,130... | collective-permute-start | bytes 98312 | tf_op jit(solution)/shard_map/ppermute | solution.py:16
  54.1 10.3 %collective-permute-start = (f32[16,128,1]{1,0,2:T(8,128)S(1)}, f32[16,128,1]{1,0,2:T(8,128)S(1)}, u32[]{:S(2)}, u32[]{:S(2)}) collective-permute-start(f32[16,128,1]{1,0,2:T(8,128)S(1)} %copy.133), channel_id=1, source_target_pairs={{0,64},{64,128},{128,192},{1,65},{65,129},{129,193},{2,66},{66,130... | collective-permute-start | bytes 24584 | tf_op jit(solution)/shard_map/ppermute | solution.py:16
  65.1 124.9 %collective-permute-start.2 = (f32[1,128,258]{1,2,0:T(8,128)}, f32[1,128,258]{1,2,0:T(8,128)S(1)}, u32[]{:S(2)}, u32[]{:S(2)}) collective-permute-start(f32[1,128,258]{1,2,0:T(8,128)} %get-tuple-element.41), channel_id=1, source_target_pairs={{2,0},{4,2},{6,4},{8,6},{10,8},{12,10},{14,12},{16,14},{18,16},{20... | collective-permute-start | bytes 396296 | tf_op jit(solution)/shard_map/ppermute | solution.py:19
  68.0 122.0 %collective-permute-start.3 = (f32[1,128,258]{1,2,0:T(8,128)}, f32[1,128,258]{1,2,0:T(8,128)}, u32[]{:S(2)}, u32[]{:S(2)}) collective-permute-start(f32[1,128,258]{1,2,0:T(8,128)} %get-tuple-element.40), channel_id=1, source_target_pairs={{0,2},{2,4},{4,6},{6,8},{8,10},{10,12},{12,14},{14,16},{16,18},{18... | collective-permute-start | bytes 396296 | tf_op jit(solution)/shard_map/ppermute | solution.py:16
  74.1 70.1 %collective-permute-start.14 = (f32[66,1,256]{2,0,1:T(8,128)S(1)}, f32[66,1,256]{2,0,1:T(8,128)S(1)}, u32[]{:S(2)}, u32[]{:S(2)}) collective-permute-start(f32[66,1,256]{2,0,1:T(8,128)S(1)} %get-tuple-element.37), channel_id=1, source_target_pairs={{2,0},{4,2},{6,4},{8,6},{10,8},{12,10},{14,12},{16,14},{18,16},{20... | collective-permute-start | bytes 202760 | tf_op jit(solution)/shard_map/ppermute | solution.py:19
  76.1 68.1 %collective-permute-start.15 = (f32[66,1,256]{2,0,1:T(8,128)S(1)}, f32[66,1,256]{2,0,1:T(8,128)S(1)}, u32[]{:S(2)}, u32[]{:S(2)}) collective-permute-start(f32[66,1,256]{2,0,1:T(8,128)S(1)} %get-tuple-element.36), channel_id=1, source_target_pairs={{0,2},{2,4},{4,6},{6,8},{8,10},{10,12},{12,14},{14,16},{16,18},{18... | collective-permute-start | bytes 202760 | tf_op jit(solution)/shard_map/ppermute | solution.py:16
  106.8 53.8 %all-to-all-start.1 = ((f32[32,128,1]{1,2,0:T(1,128)}), f32[32,128,1]{1,2,0:T(1,128)S(1)}, u32[]{:S(2)}, u32[]{:S(2)}) async-start(f32[32,128,1]{1,2,0:T(1,128)} %bitcast.19), calls=%async_computation.1 | async-start | bytes 32768 | tf_op jit(solution)/shard_map/all_to_all | solution.py:87
  151.1 21.3 %collective-permute-start.16 = (f32[66,34,1]{0,1,2:T(8,128)}, f32[66,34,1]{0,1,2:T(8,128)}, u32[]{:S(2)}, u32[]{:S(2)}) collective-permute-start(f32[66,34,1]{0,1,2:T(8,128)} %copy.119), channel_id=1, source_target_pairs={{1,0},{3,2},{5,4},{7,6},{9,8},{11,10},{13,12},{15,14},{17,16},{19,... | collective-permute-start | bytes 26936 | tf_op jit(solution)/shard_map/ppermute | solution.py:19
  153.6 20.2 %collective-permute-start.17 = (f32[66,34,1]{0,1,2:T(8,128)}, f32[66,34,1]{0,1,2:T(8,128)}, u32[]{:S(2)}, u32[]{:S(2)}) collective-permute-start(f32[66,34,1]{0,1,2:T(8,128)} %copy.121), channel_id=1, source_target_pairs={{0,1},{2,3},{4,5},{6,7},{8,9},{10,11},{12,13},{14,15},{16,17},{18,... | collective-permute-start | bytes 26936 | tf_op jit(solution)/shard_map/ppermute | solution.py:16
  197.0 16.4 %collective-permute-start.4 = (f32[18,1,258]{2,0,1:T(8,128)S(1)}, f32[18,1,258]{2,0,1:T(8,128)S(1)}, u32[]{:S(2)}, u32[]{:S(2)}) collective-permute-start(f32[18,1,258]{2,0,1:T(8,128)S(1)} %copy.86), channel_id=1, source_target_pairs={{1,0},{3,2},{5,4},{7,6},{9,8},{11,10},{13,12},{15,14},{17,16},{19,... | collective-permute-start | bytes 55736 | tf_op jit(solution)/shard_map/ppermute | solution.py:19
  201.4 14.4 %collective-permute-start.5 = (f32[18,1,258]{2,0,1:T(8,128)S(1)}, f32[18,1,258]{2,0,1:T(8,128)S(1)}, u32[]{:S(2)}, u32[]{:S(2)}) collective-permute-start(f32[18,1,258]{2,0,1:T(8,128)S(1)} %copy.88), channel_id=1, source_target_pairs={{0,1},{2,3},{4,5},{6,7},{8,9},{10,11},{12,13},{14,15},{16,17},{18,... | collective-permute-start | bytes 55736 | tf_op jit(solution)/shard_map/ppermute | solution.py:16
  205.5 27.5 %collective-permute-start.18 = (f32[1,32,256]{2,0,1:T(1,128)S(1)}, f32[1,32,256]{2,0,1:T(1,128)S(1)}, u32[]{:S(2)}, u32[]{:S(2)}) collective-permute-start(f32[1,32,256]{2,0,1:T(1,128)S(1)} %get-tuple-element.43), channel_id=1, source_target_pairs={{64,0},{128,64},{192,128},{65,1},{129,65},{193,129},{66,2},{130,66... | collective-permute-start | bytes 98312 | tf_op jit(solution)/shard_map/ppermute | solution.py:19
  207.4 25.6 %collective-permute-start.19 = (f32[1,32,256]{2,0,1:T(1,128)S(1)}, f32[1,32,256]{2,0,1:T(1,128)S(1)}, u32[]{:S(2)}, u32[]{:S(2)}) collective-permute-start(f32[1,32,256]{2,0,1:T(1,128)S(1)} %get-tuple-element.42), channel_id=1, source_target_pairs={{0,64},{64,128},{128,192},{1,65},{65,129},{129,193},{2,66},{66,130... | collective-permute-start | bytes 98312 | tf_op jit(solution)/shard_map/ppermute | solution.py:16
  226.2 15.7 %collective-permute-start.6 = (f32[16,128,1]{1,0,2:T(8,128)S(1)}, f32[16,128,1]{1,0,2:T(8,128)S(1)}, u32[]{:S(2)}, u32[]{:S(2)}) collective-permute-start(f32[16,128,1]{1,0,2:T(8,128)S(1)} %bitcast.91), channel_id=1, source_target_pairs={{0,64},{64,128},{128,192},{1,65},{65,129},{129,193},{2,66},{66,130... | collective-permute-start | bytes 24584 | tf_op jit(solution)/shard_map/ppermute | solution.py:16
  228.2 13.8 %collective-permute-start.7 = (f32[16,128,1]{1,0,2:T(8,128)S(1)}, f32[16,128,1]{1,0,2:T(8,128)S(1)}, u32[]{:S(2)}, u32[]{:S(2)}) collective-permute-start(f32[16,128,1]{1,0,2:T(8,128)S(1)} %bitcast.90), channel_id=1, source_target_pairs={{64,0},{128,64},{192,128},{65,1},{129,65},{193,129},{66,2},{130,66... | collective-permute-start | bytes 24584 | tf_op jit(solution)/shard_map/ppermute | solution.py:19
  233.1 18.5 %collective-permute-start.20 = (f32[66,1,256]{2,0,1:T(8,128)S(1)}, f32[66,1,256]{2,0,1:T(8,128)S(1)}, u32[]{:S(2)}, u32[]{:S(2)}) collective-permute-start(f32[66,1,256]{2,0,1:T(8,128)S(1)} %get-tuple-element.35), channel_id=1, source_target_pairs={{2,0},{4,2},{6,4},{8,6},{10,8},{12,10},{14,12},{16,14},{18,16},{20... | collective-permute-start | bytes 202760 | tf_op jit(solution)/shard_map/ppermute | solution.py:19
  235.8 15.8 %collective-permute-start.21 = (f32[66,1,256]{2,0,1:T(8,128)S(1)}, f32[66,1,256]{2,0,1:T(8,128)S(1)}, u32[]{:S(2)}, u32[]{:S(2)}) collective-permute-start(f32[66,1,256]{2,0,1:T(8,128)S(1)} %get-tuple-element.34), channel_id=1, source_target_pairs={{0,2},{2,4},{4,6},{6,8},{8,10},{10,12},{12,14},{14,16},{16,18},{18... | collective-permute-start | bytes 202760 | tf_op jit(solution)/shard_map/ppermute | solution.py:16
  242.7 24.0 %collective-permute-start.8 = (f32[1,128,258]{1,2,0:T(8,128)}, f32[1,128,258]{1,2,0:T(8,128)S(1)}, u32[]{:S(2)}, u32[]{:S(2)}) collective-permute-start(f32[1,128,258]{1,2,0:T(8,128)} %get-tuple-element.39), channel_id=1, source_target_pairs={{2,0},{4,2},{6,4},{8,6},{10,8},{12,10},{14,12},{16,14},{18,16},{20... | collective-permute-start | bytes 396296 | tf_op jit(solution)/shard_map/ppermute | solution.py:19
  244.6 22.1 %collective-permute-start.9 = (f32[1,128,258]{1,2,0:T(8,128)}, f32[1,128,258]{1,2,0:T(8,128)}, u32[]{:S(2)}, u32[]{:S(2)}) collective-permute-start(f32[1,128,258]{1,2,0:T(8,128)} %get-tuple-element.38), channel_id=1, source_target_pairs={{0,2},{2,4},{4,6},{6,8},{8,10},{10,12},{12,14},{14,16},{16,18},{18... | collective-permute-start | bytes 396296 | tf_op jit(solution)/shard_map/ppermute | solution.py:16
  275.2 26.1 %collective-permute-start.10 = (f32[18,1,258]{2,0,1:T(8,128)}, f32[18,1,258]{2,0,1:T(8,128)}, u32[]{:S(2)}, u32[]{:S(2)}) collective-permute-start(f32[18,1,258]{2,0,1:T(8,128)} %copy.105), channel_id=1, source_target_pairs={{1,0},{3,2},{5,4},{7,6},{9,8},{11,10},{13,12},{15,14},{17,16},{19,... | collective-permute-start | bytes 55736 | tf_op jit(solution)/shard_map/ppermute | solution.py:19
  280.1 24.2 %collective-permute-start.11 = (f32[18,1,258]{2,0,1:T(8,128)}, f32[18,1,258]{2,0,1:T(8,128)}, u32[]{:S(2)}, u32[]{:S(2)}) collective-permute-start(f32[18,1,258]{2,0,1:T(8,128)} %copy.107), channel_id=1, source_target_pairs={{0,1},{2,3},{4,5},{6,7},{8,9},{10,11},{12,13},{14,15},{16,17},{18,... | collective-permute-start | bytes 55736 | tf_op jit(solution)/shard_map/ppermute | solution.py:16
  (20 other events, 405.1 us)
where the time goes:
time: 323 us; the launch traced here: 322 us
  local copies, waits for them, and re-layouts  116 us (36%)
  starting transfers between devices  102 us (32%)
  other arithmetic  102 us (32%)
    ppermute x12, starting transfers between devices, padded_2(): lax.ppermute(lax.slice_in_dim(block, block.shape[dim] - width, None, axis...  60.5 us
    scatter-add x1, other arithmetic, local(): jax.ops.segment_sum(heat_flux, safe_targets, num_segments=fin_width * fin...  29.4 us
    ppermute x12, starting transfers between devices, padded_2(): lax.ppermute(lax.slice_in_dim(block, 0, width, axis=dim), axis, backward)  25.2 us
    gather x1, local copies, waits for them, and re-layouts, local(): fin_wall = jnp.where(valid, surface[safe_targets], 0.0)  23 us
    slice x10, local copies, waits for them, and re-layouts, padded_2(): lax.slice_in_dim(block, 0, width, axis=dim)  21.7 us
    select_n x2, other arithmetic, fluid_update(): return jnp.where(update_mask, updated, field)  19.7 us
    add x1, other arithmetic, local(): omega * (first_state + (fin_rhs - second_image) / diag - fin_temp)  14.3 us
    add x1, other arithmetic, local(): first_state = fin_temp + (fin_rhs - fin_image(fin_temp)) / diag  13.9 us
  transfers between devices with their start and end apart: 26, of which 0 were waited for; matrix products, arithmetic and copies ran while one was open for 56% of the time, Pallas kernels for 0%

commit v1 on v0

--- a/solution.py
+++ b/solution.py
@@ -74,8 +74,17 @@
         .at[slot_index]
         .set(targets.astype(jnp.float32))
     )
-    received = lax.all_to_all(
-        jnp.stack([send_temps, send_targets]), "gx", split_axis=1, concat_axis=1, tiled=True
+    received = jnp.concatenate(
+        jax.lax.all_to_all(
+            jnp.stack(
+                jnp.split(jnp.stack([send_temps, send_targets]), jax.lax.axis_size("gx"), axis=1),
+                axis=0,
+            ),
+            axis_name="gx",
+            concat_axis=0,
+            split_axis=0,
+        ),
+        axis=1,
     )
     got_targets = received[1].astype(jnp.int32)
     valid = (got_targets >= 0) & on_wall

time: 323 us -> 341 us (1.056)
  other arithmetic: 102 us -> 120 us
    unnamed x0 -> x31, other arithmetic: none -> 17.8 us
  transfers between devices with their start and end apart: 26 -> 26, of which waited for: 0 -> 0; matrix products, arithmetic and copies ran while one was open for 56% -> 58% of each run, Pallas kernels for 0% -> 0%
where the time goes in v1:
time: 341 us; the launch traced here: 340 us
  other arithmetic  120 us (35%)
  local copies, waits for them, and re-layouts  116 us (34%)
  starting transfers between devices  102 us (30%)
    ppermute x12, starting transfers between devices, padded_2(): lax.ppermute(lax.slice_in_dim(block, block.shape[dim] - width, None, axis...  60.5 us
    scatter-add x1, other arithmetic, local(): jax.ops.segment_sum(heat_flux, safe_targets, num_segments=fin_width * fin...  29.4 us
    ppermute x12, starting transfers between devices, padded_2(): lax.ppermute(lax.slice_in_dim(block, 0, width, axis=dim), axis, backward)  25.1 us
    gather x1, local copies, waits for them, and re-layouts, local(): fin_wall = jnp.where(valid, surface[safe_targets], 0.0)  23 us
    slice x10, local copies, waits for them, and re-layouts, padded_2(): lax.slice_in_dim(block, 0, width, axis=dim)  21.7 us
    select_n x2, other arithmetic, fluid_update(): return jnp.where(update_mask, updated, field)  19.8 us
    unnamed x31, other arithmetic  17.8 us
    add x1, other arithmetic, local(): omega * (first_state + (fin_rhs - second_image) / diag - fin_temp)  14.5 us
  transfers between devices with their start and end apart: 26, of which 0 were waited for; matrix products, arithmetic and copies ran while one was open for 58% of the time, Pallas kernels for 0%

profile of v1, /device:TPU:120, one launch (start us, length us, event | category | flops | bytes accessed | tf_op | source)
XLA Modules:
  0.0 339.6 jit_solution(6874252307558144011)
XLA Ops:
  4.9 9.1 %reduce-window.6 = s32[32,16,128]{2,1,0:T(8,128)S(1)} reduce-window(s32[32,16,128]{2,1,0:T(8,128)S(1)} %fusion.41, s32[]{:T(128)} %constant.65.clone.1), window={size=1x1x128 pad=0_0x0_0x127_0}, to_apply=%region_0.0 | reduce-window | flops 8323072 | bytes 524292 | tf_op jit(solution)/shard_map/reduce-window
  14.8 8.1 %scatter_custom_fusion = f32[4096]{0:T(1024)S(1)} fusion(s32[2048]{0:T(1024)S(1)} %bitcast.218, f32[2048]{0:T(1024)S(1)} %bitcast.222, f32[]{:T(128)} %constant.70.clone.1), kind=kCustom, calls=%fused_computation.257 | custom fusion | bytes 16388 | tf_op jit(solution)/shard_map/scatter | solution.py:71
  22.9 8.1 %scatter_custom_fusion.1 = f32[4096]{0:T(1024)S(1)} fusion(s32[2048]{0:T(1024)S(1)} %bitcast.219, f32[2048]{0:T(1024)S(1)} %bitcast.223, f32[]{:T(128)} %constant.73.clone.1), kind=kCustom, calls=%fused_computation.255 | custom fusion | bytes 16388 | tf_op jit(solution)/shard_map/scatter | solution.py:75
  49.4 8.2 %all-to-all-start = ((f32[32,2,128]{2,1,0:T(2,128)}), f32[32,2,128]{2,1,0:T(2,128)S(1)}, u32[]{:S(2)}, u32[]{:S(2)}) async-start(f32[32,2,128]{2,1,0:T(2,128)} %constant_dynamic-update-slice_fusion), calls=%async_computation | async-start | bytes 65536 | tf_op jit(solution)/shard_map/all_to_all | solution.py:78
  57.6 5.9 %copy_add_fusion = (f32[64,32,256]{2,0,1:T(8,128)}, f32[64,32,256]{2,0,1:T(8,128)S(1)}) fusion(f32[64,32,256]{2,1,0:T(8,128)} %param.11, f32[64,32,256]{2,1,0:T(8,128)} %param.10), kind=kLoop, calls=%fused_computation.124 | loop fusion | flops 524288 | bytes 8388608 | tf_op jit(solution)/shard_map/add | solution.py:98
  65.5 6.0 %collective-permute-start.13 = (f32[1,32,256]{2,0,1:T(1,128)S(1)}, f32[1,32,256]{2,0,1:T(1,128)S(1)}, u32[]{:S(2)}, u32[]{:S(2)}) collective-permute-start(f32[1,32,256]{2,0,1:T(1,128)S(1)} %copy.114), channel_id=1, source_target_pairs={{0,64},{64,128},{128,192},{1,65},{65,129},{129,193},{2,66},{66,130... | collective-permute-start | bytes 98312 | tf_op jit(solution)/shard_map/ppermute | solution.py:16
  71.9 4.8 %collective-permute-start = (f32[16,128,1]{1,0,2:T(8,128)S(1)}, f32[16,128,1]{1,0,2:T(8,128)S(1)}, u32[]{:S(2)}, u32[]{:S(2)}) collective-permute-start(f32[16,128,1]{1,0,2:T(8,128)S(1)} %copy.131), channel_id=1, source_target_pairs={{0,64},{64,128},{128,192},{1,65},{65,129},{129,193},{2,66},{66,130... | collective-permute-start | bytes 24584 | tf_op jit(solution)/shard_map/ppermute | solution.py:16
  85.6 6.1 %collective-permute-start.3 = (f32[1,128,258]{1,2,0:T(8,128)}, f32[1,128,258]{1,2,0:T(8,128)}, u32[]{:S(2)}, u32[]{:S(2)}) collective-permute-start(f32[1,128,258]{1,2,0:T(8,128)} %get-tuple-element.38), channel_id=1, source_target_pairs={{0,2},{2,4},{4,6},{6,8},{8,10},{10,12},{12,14},{14,16},{16,18},{18... | collective-permute-start | bytes 396296 | tf_op jit(solution)/shard_map/ppermute | solution.py:16
  93.7 6.9 %collective-permute-start.15 = (f32[66,1,256]{2,0,1:T(8,128)S(1)}, f32[66,1,256]{2,0,1:T(8,128)S(1)}, u32[]{:S(2)}, u32[]{:S(2)}) collective-permute-start(f32[66,1,256]{2,0,1:T(8,128)S(1)} %get-tuple-element.34), channel_id=1, source_target_pairs={{0,2},{2,4},{4,6},{6,8},{8,10},{10,12},{12,14},{14,16},{16,18},{18... | collective-permute-start | bytes 202760 | tf_op jit(solution)/shard_map/ppermute | solution.py:16
  100.7 23.0 %gather_fusion = f32[4096]{0:T(1024)S(1)} fusion(f32[8192]{0:T(1024)S(1)} %bitcast.127, s32[4096]{0:T(1024)S(1)} %broadcast_clamp_fusion), kind=kCustom, calls=%fused_computation | custom fusion | bytes 49152 | tf_op jit(solution)/shard_map/gather | solution.py:93
  124.4 8.0 %all-to-all-start.1 = ((f32[32,128,1]{1,2,0:T(1,128)}), f32[32,128,1]{1,2,0:T(1,128)S(1)}, u32[]{:S(2)}, u32[]{:S(2)}) async-start(f32[32,128,1]{1,2,0:T(1,128)} %bitcast.52), calls=%async_computation.1 | async-start | bytes 32768 | tf_op jit(solution)/shard_map/all_to_all | solution.py:96
  132.4 29.4 %scatter_custom_fusion.2 = f32[8192]{0:T(1024)} fusion(s32[4096]{0:T(1024)S(1)} %bitcast.221, f32[4096]{0:T(1024)S(1)} %get-tuple-element.18, f32[]{:T(128)} %constant.70.clone.1), kind=kCustom, calls=%fused_computation.250 | custom fusion | flops 4096 | bytes 32772 | tf_op jit(solution)/shard_map/scatter-add | solution.py:95
  171.1 4.2 %collective-permute-start.17 = (f32[66,34,1]{0,1,2:T(8,128)}, f32[66,34,1]{0,1,2:T(8,128)}, u32[]{:S(2)}, u32[]{:S(2)}) collective-permute-start(f32[66,34,1]{0,1,2:T(8,128)} %copy.119), channel_id=1, source_target_pairs={{0,1},{2,3},{4,5},{6,7},{8,9},{10,11},{12,13},{14,15},{16,17},{18,... | collective-permute-start | bytes 26936 | tf_op jit(solution)/shard_map/ppermute | solution.py:16
  178.1 11.9 %gather_fusion.1 = f32[2048]{0:T(1024)S(1)} fusion(f32[4096]{0:T(1024)S(1)} %bitcast.128, s32[2048]{0:T(1024)} %broadcast_clamp_fusion.1), kind=kCustom, calls=%fused_computation.1 | custom fusion | bytes 24576 | tf_op jit(solution)/shard_map/gather | solution.py:97
  193.6 13.9 %fusion.23 = f32[64,32,256]{2,0,1:T(8,128)} fusion(f32[64,32,256]{2,0,1:T(8,128)} %copy-done.1, f32[64,32,256]{2,0,1:T(8,128)} %scatter-add.13, f32[66,34,1]{2,0,1:T(8,128)} %copy.120, f32[66,1,256]{2,0,1:T(8,128)} %copy-done.7, f32[66,1,256]{2,0,1:T(8,128)} %copy-done.8, f32[1,32,256]{2,0,1:T(1,128)S(1)} %collective-permute-done.12, ...), kind=kLoop, calls=%fused_computation.56 | loop fusion | flops 14680064 | bytes 6510112 | tf_op jit(solution)/shard_map/add | solution.py:111
  225.0 6.0 %collective-permute-start.19 = (f32[1,32,256]{2,0,1:T(1,128)S(1)}, f32[1,32,256]{2,0,1:T(1,128)S(1)}, u32[]{:S(2)}, u32[]{:S(2)}) collective-permute-start(f32[1,32,256]{2,0,1:T(1,128)S(1)} %get-tuple-element.40), channel_id=1, source_target_pairs={{0,64},{64,128},{128,192},{1,65},{65,129},{129,193},{2,66},{66,130... | collective-permute-start | bytes 98312 | tf_op jit(solution)/shard_map/ppermute | solution.py:16
  235.6 8.2 %fusion.2 = (f32[16,128,256]{1,2,0:T(8,128)S(1)}, pred[16,128,256]{1,2,0:T(8,128)(4,1)}) fusion(f32[16,128,256]{1,2,0:T(8,128)S(1)} %copy.109, f32[16,128,1]{1,2,0:T(1,128)S(1)} %bitcast.202, f32[16,128,1]{1,2,0:T(1,128)S(1)} %bitcast.199, f32[18,1,258]{1,2,0:T(8,128)} %copy.87, f32[1,128,258]{1,2,0:T(8,128)S(1)} %collective-permute-done.2, ...), kind=kLoop, calls=%fused_computation.16 | loop fusion | flops 23068672 | bytes 7141920 | tf_op jit(solution)/shard_map/jit(_where)/select_n | solution.py:53
  245.8 4.8 %collective-permute-start.7 = (f32[16,128,1]{1,0,2:T(8,128)S(1)}, f32[16,128,1]{1,0,2:T(8,128)S(1)}, u32[]{:S(2)}, u32[]{:S(2)}) collective-permute-start(f32[16,128,1]{1,0,2:T(8,128)S(1)} %bitcast.224), channel_id=1, source_target_pairs={{64,0},{128,64},{192,128},{65,1},{129,65},{193,129},{66,2},{130,66... | collective-permute-start | bytes 24584 | tf_op jit(solution)/shard_map/ppermute | solution.py:19
  253.4 6.1 %collective-permute-start.21 = (f32[66,1,256]{2,0,1:T(8,128)S(1)}, f32[66,1,256]{2,0,1:T(8,128)S(1)}, u32[]{:S(2)}, u32[]{:S(2)}) collective-permute-start(f32[66,1,256]{2,0,1:T(8,128)S(1)} %get-tuple-element.32), channel_id=1, source_target_pairs={{0,2},{2,4},{4,6},{6,8},{8,10},{10,12},{12,14},{14,16},{16,18},{18... | collective-permute-start | bytes 202760 | tf_op jit(solution)/shard_map/ppermute | solution.py:16
  262.2 6.9 %collective-permute-start.9 = (f32[1,128,258]{1,2,0:T(8,128)}, f32[1,128,258]{1,2,0:T(8,128)}, u32[]{:S(2)}, u32[]{:S(2)}) collective-permute-start(f32[1,128,258]{1,2,0:T(8,128)} %get-tuple-element.36), channel_id=1, source_target_pairs={{0,2},{2,4},{4,6},{6,8},{8,10},{10,12},{12,14},{14,16},{16,18},{18... | collective-permute-start | bytes 396296 | tf_op jit(solution)/shard_map/ppermute | solution.py:16
  276.5 4.2 %collective-permute-start.23 = (f32[66,34,1]{0,1,2:T(8,128)}, f32[66,34,1]{0,1,2:T(8,128)}, u32[]{:S(2)}, u32[]{:S(2)}) collective-permute-start(f32[66,34,1]{0,1,2:T(8,128)} %copy.124), channel_id=1, source_target_pairs={{0,1},{2,3},{4,5},{6,7},{8,9},{10,11},{12,13},{14,15},{16,17},{18,... | collective-permute-start | bytes 26936 | tf_op jit(solution)/shard_map/ppermute | solution.py:16
  297.8 4.2 %collective-permute-start.11 = (f32[18,1,258]{2,0,1:T(8,128)}, f32[18,1,258]{2,0,1:T(8,128)}, u32[]{:S(2)}, u32[]{:S(2)}) collective-permute-start(f32[18,1,258]{2,0,1:T(8,128)} %copy.105), channel_id=1, source_target_pairs={{0,1},{2,3},{4,5},{6,7},{8,9},{10,11},{12,13},{14,15},{16,17},{18,... | collective-permute-start | bytes 55736 | tf_op jit(solution)/shard_map/ppermute | solution.py:16
  302.0 14.5 %fusion.14 = f32[64,32,256]{2,0,1:T(8,128)S(1)} fusion(f32[64,32,256]{2,0,1:T(8,128)} %fusion.23, f32[64,32,256]{2,0,1:T(8,128)} %scatter-add.13, f32[66,34,1]{2,0,1:T(8,128)} %copy.125, f32[66,1,256]{2,0,1:T(8,128)} %copy-done.9, f32[66,1,256]{2,0,1:T(8,128)} %copy-done.10, f32[1,32,256]{2,0,1:T(1,128)S(1)} %collective-permute-done.18, ...), kind=kLoop, calls=%fused_computation.29 | loop fusion | flops 16252928 | bytes 8607264 | tf_op jit(solution)/shard_map/add | solution.py:119
  325.2 11.5 %fusion.5 = f32[16,128,256]{1,2,0:T(8,128)} fusion(f32[16,128,256]{1,2,0:T(8,128)} %copy-done.3, f32[16,128,256]{1,2,0:T(8,128)S(1)} %copy.109, f32[16,128,1]{1,2,0:T(1,128)S(1)} %bitcast.205, f32[16,128,1]{1,2,0:T(1,128)S(1)} %bitcast.208, f32[18,1,258]{1,2,0:T(8,128)} %copy.106, f32[1,128,258]{1,2,0:T(8,128)S(1)} %collective-permute-done.8, ...), kind=kLoop, calls=%fused_computation.19 | loop fusion | flops 22544384 | bytes 7141920 | tf_op jit(solution)/shard_map/jit(_where)/select_n | solution.py:53
  (164 shorter events, 118.1 us)
Async XLA Ops:
  2.9 79.2 %collective-permute-start.1 = (f32[16,128,1]{1,0,2:T(8,128)S(1)}, f32[16,128,1]{1,0,2:T(8,128)S(1)}, u32[]{:S(2)}, u32[]{:S(2)}) collective-permute-start(f32[16,128,1]{1,0,2:T(8,128)S(1)} %copy.132), channel_id=1, source_target_pairs={{64,0},{128,64},{192,128},{65,1},{129,65},{193,129},{66,2},{130,66... | collective-permute-start | bytes 24584 | tf_op jit(solution)/shard_map/ppermute | solution.py:19
  49.4 51.3 %all-to-all-start = ((f32[32,2,128]{2,1,0:T(2,128)}), f32[32,2,128]{2,1,0:T(2,128)S(1)}, u32[]{:S(2)}, u32[]{:S(2)}) async-start(f32[32,2,128]{2,1,0:T(2,128)} %constant_dynamic-update-slice_fusion), calls=%async_computation | async-start | bytes 65536 | tf_op jit(solution)/shard_map/all_to_all | solution.py:78
  63.5 28.2 %collective-permute-start.12 = (f32[1,32,256]{2,0,1:T(1,128)S(1)}, f32[1,32,256]{2,0,1:T(1,128)S(1)}, u32[]{:S(2)}, u32[]{:S(2)}) collective-permute-start(f32[1,32,256]{2,0,1:T(1,128)S(1)} %slice.268), channel_id=1, source_target_pairs={{64,0},{128,64},{192,128},{65,1},{129,65},{193,129},{66,2},{130,66... | collective-permute-start | bytes 98312 | tf_op jit(solution)/shard_map/ppermute | solution.py:19
  65.5 26.2 %collective-permute-start.13 = (f32[1,32,256]{2,0,1:T(1,128)S(1)}, f32[1,32,256]{2,0,1:T(1,128)S(1)}, u32[]{:S(2)}, u32[]{:S(2)}) collective-permute-start(f32[1,32,256]{2,0,1:T(1,128)S(1)} %copy.114), channel_id=1, source_target_pairs={{0,64},{64,128},{128,192},{1,65},{65,129},{129,193},{2,66},{66,130... | collective-permute-start | bytes 98312 | tf_op jit(solution)/shard_map/ppermute | solution.py:16
  71.9 10.3 %collective-permute-start = (f32[16,128,1]{1,0,2:T(8,128)S(1)}, f32[16,128,1]{1,0,2:T(8,128)S(1)}, u32[]{:S(2)}, u32[]{:S(2)}) collective-permute-start(f32[16,128,1]{1,0,2:T(8,128)S(1)} %copy.131), channel_id=1, source_target_pairs={{0,64},{64,128},{128,192},{1,65},{65,129},{129,193},{2,66},{66,130... | collective-permute-start | bytes 24584 | tf_op jit(solution)/shard_map/ppermute | solution.py:16
  82.8 124.7 %collective-permute-start.2 = (f32[1,128,258]{1,2,0:T(8,128)}, f32[1,128,258]{1,2,0:T(8,128)S(1)}, u32[]{:S(2)}, u32[]{:S(2)}) collective-permute-start(f32[1,128,258]{1,2,0:T(8,128)} %get-tuple-element.39), channel_id=1, source_target_pairs={{2,0},{4,2},{6,4},{8,6},{10,8},{12,10},{14,12},{16,14},{18,16},{20... | collective-permute-start | bytes 396296 | tf_op jit(solution)/shard_map/ppermute | solution.py:19
  85.6 121.9 %collective-permute-start.3 = (f32[1,128,258]{1,2,0:T(8,128)}, f32[1,128,258]{1,2,0:T(8,128)}, u32[]{:S(2)}, u32[]{:S(2)}) collective-permute-start(f32[1,128,258]{1,2,0:T(8,128)} %get-tuple-element.38), channel_id=1, source_target_pairs={{0,2},{2,4},{4,6},{6,8},{8,10},{10,12},{12,14},{14,16},{16,18},{18... | collective-permute-start | bytes 396296 | tf_op jit(solution)/shard_map/ppermute | solution.py:16
  91.8 70.0 %collective-permute-start.14 = (f32[66,1,256]{2,0,1:T(8,128)S(1)}, f32[66,1,256]{2,0,1:T(8,128)S(1)}, u32[]{:S(2)}, u32[]{:S(2)}) collective-permute-start(f32[66,1,256]{2,0,1:T(8,128)S(1)} %get-tuple-element.35), channel_id=1, source_target_pairs={{2,0},{4,2},{6,4},{8,6},{10,8},{12,10},{14,12},{16,14},{18,16},{20... | collective-permute-start | bytes 202760 | tf_op jit(solution)/shard_map/ppermute | solution.py:19
  93.7 68.1 %collective-permute-start.15 = (f32[66,1,256]{2,0,1:T(8,128)S(1)}, f32[66,1,256]{2,0,1:T(8,128)S(1)}, u32[]{:S(2)}, u32[]{:S(2)}) collective-permute-start(f32[66,1,256]{2,0,1:T(8,128)S(1)} %get-tuple-element.34), channel_id=1, source_target_pairs={{0,2},{2,4},{4,6},{6,8},{8,10},{10,12},{12,14},{14,16},{16,18},{18... | collective-permute-start | bytes 202760 | tf_op jit(solution)/shard_map/ppermute | solution.py:16
  124.4 53.7 %all-to-all-start.1 = ((f32[32,128,1]{1,2,0:T(1,128)}), f32[32,128,1]{1,2,0:T(1,128)S(1)}, u32[]{:S(2)}, u32[]{:S(2)}) async-start(f32[32,128,1]{1,2,0:T(1,128)} %bitcast.52), calls=%async_computation.1 | async-start | bytes 32768 | tf_op jit(solution)/shard_map/all_to_all | solution.py:96
  168.7 21.3 %collective-permute-start.16 = (f32[66,34,1]{0,1,2:T(8,128)}, f32[66,34,1]{0,1,2:T(8,128)}, u32[]{:S(2)}, u32[]{:S(2)}) collective-permute-start(f32[66,34,1]{0,1,2:T(8,128)} %copy.117), channel_id=1, source_target_pairs={{1,0},{3,2},{5,4},{7,6},{9,8},{11,10},{13,12},{15,14},{17,16},{19,... | collective-permute-start | bytes 26936 | tf_op jit(solution)/shard_map/ppermute | solution.py:19
  171.1 20.2 %collective-permute-start.17 = (f32[66,34,1]{0,1,2:T(8,128)}, f32[66,34,1]{0,1,2:T(8,128)}, u32[]{:S(2)}, u32[]{:S(2)}) collective-permute-start(f32[66,34,1]{0,1,2:T(8,128)} %copy.119), channel_id=1, source_target_pairs={{0,1},{2,3},{4,5},{6,7},{8,9},{10,11},{12,13},{14,15},{16,17},{18,... | collective-permute-start | bytes 26936 | tf_op jit(solution)/shard_map/ppermute | solution.py:16
  214.6 16.4 %collective-permute-start.4 = (f32[18,1,258]{2,0,1:T(8,128)S(1)}, f32[18,1,258]{2,0,1:T(8,128)S(1)}, u32[]{:S(2)}, u32[]{:S(2)}) collective-permute-start(f32[18,1,258]{2,0,1:T(8,128)S(1)} %copy.84), channel_id=1, source_target_pairs={{1,0},{3,2},{5,4},{7,6},{9,8},{11,10},{13,12},{15,14},{17,16},{19,... | collective-permute-start | bytes 55736 | tf_op jit(solution)/shard_map/ppermute | solution.py:19
  218.9 14.4 %collective-permute-start.5 = (f32[18,1,258]{2,0,1:T(8,128)S(1)}, f32[18,1,258]{2,0,1:T(8,128)S(1)}, u32[]{:S(2)}, u32[]{:S(2)}) collective-permute-start(f32[18,1,258]{2,0,1:T(8,128)S(1)} %copy.86), channel_id=1, source_target_pairs={{0,1},{2,3},{4,5},{6,7},{8,9},{10,11},{12,13},{14,15},{16,17},{18,... | collective-permute-start | bytes 55736 | tf_op jit(solution)/shard_map/ppermute | solution.py:16
  223.1 27.5 %collective-permute-start.18 = (f32[1,32,256]{2,0,1:T(1,128)S(1)}, f32[1,32,256]{2,0,1:T(1,128)S(1)}, u32[]{:S(2)}, u32[]{:S(2)}) collective-permute-start(f32[1,32,256]{2,0,1:T(1,128)S(1)} %get-tuple-element.41), channel_id=1, source_target_pairs={{64,0},{128,64},{192,128},{65,1},{129,65},{193,129},{66,2},{130,66... | collective-permute-start | bytes 98312 | tf_op jit(solution)/shard_map/ppermute | solution.py:19
  225.0 25.6 %collective-permute-start.19 = (f32[1,32,256]{2,0,1:T(1,128)S(1)}, f32[1,32,256]{2,0,1:T(1,128)S(1)}, u32[]{:S(2)}, u32[]{:S(2)}) collective-permute-start(f32[1,32,256]{2,0,1:T(1,128)S(1)} %get-tuple-element.40), channel_id=1, source_target_pairs={{0,64},{64,128},{128,192},{1,65},{65,129},{129,193},{2,66},{66,130... | collective-permute-start | bytes 98312 | tf_op jit(solution)/shard_map/ppermute | solution.py:16
  243.8 15.7 %collective-permute-start.6 = (f32[16,128,1]{1,0,2:T(8,128)S(1)}, f32[16,128,1]{1,0,2:T(8,128)S(1)}, u32[]{:S(2)}, u32[]{:S(2)}) collective-permute-start(f32[16,128,1]{1,0,2:T(8,128)S(1)} %bitcast.225), channel_id=1, source_target_pairs={{0,64},{64,128},{128,192},{1,65},{65,129},{129,193},{2,66},{66,130... | collective-permute-start | bytes 24584 | tf_op jit(solution)/shard_map/ppermute | solution.py:16
  245.8 13.8 %collective-permute-start.7 = (f32[16,128,1]{1,0,2:T(8,128)S(1)}, f32[16,128,1]{1,0,2:T(8,128)S(1)}, u32[]{:S(2)}, u32[]{:S(2)}) collective-permute-start(f32[16,128,1]{1,0,2:T(8,128)S(1)} %bitcast.224), channel_id=1, source_target_pairs={{64,0},{128,64},{192,128},{65,1},{129,65},{193,129},{66,2},{130,66... | collective-permute-start | bytes 24584 | tf_op jit(solution)/shard_map/ppermute | solution.py:19
  250.7 18.5 %collective-permute-start.20 = (f32[66,1,256]{2,0,1:T(8,128)S(1)}, f32[66,1,256]{2,0,1:T(8,128)S(1)}, u32[]{:S(2)}, u32[]{:S(2)}) collective-permute-start(f32[66,1,256]{2,0,1:T(8,128)S(1)} %get-tuple-element.33), channel_id=1, source_target_pairs={{2,0},{4,2},{6,4},{8,6},{10,8},{12,10},{14,12},{16,14},{18,16},{20... | collective-permute-start | bytes 202760 | tf_op jit(solution)/shard_map/ppermute | solution.py:19
  253.4 15.8 %collective-permute-start.21 = (f32[66,1,256]{2,0,1:T(8,128)S(1)}, f32[66,1,256]{2,0,1:T(8,128)S(1)}, u32[]{:S(2)}, u32[]{:S(2)}) collective-permute-start(f32[66,1,256]{2,0,1:T(8,128)S(1)} %get-tuple-element.32), channel_id=1, source_target_pairs={{0,2},{2,4},{4,6},{6,8},{8,10},{10,12},{12,14},{14,16},{16,18},{18... | collective-permute-start | bytes 202760 | tf_op jit(solution)/shard_map/ppermute | solution.py:16
  260.3 24.0 %collective-permute-start.8 = (f32[1,128,258]{1,2,0:T(8,128)}, f32[1,128,258]{1,2,0:T(8,128)S(1)}, u32[]{:S(2)}, u32[]{:S(2)}) collective-permute-start(f32[1,128,258]{1,2,0:T(8,128)} %get-tuple-element.37), channel_id=1, source_target_pairs={{2,0},{4,2},{6,4},{8,6},{10,8},{12,10},{14,12},{16,14},{18,16},{20... | collective-permute-start | bytes 396296 | tf_op jit(solution)/shard_map/ppermute | solution.py:19
  262.2 22.1 %collective-permute-start.9 = (f32[1,128,258]{1,2,0:T(8,128)}, f32[1,128,258]{1,2,0:T(8,128)}, u32[]{:S(2)}, u32[]{:S(2)}) collective-permute-start(f32[1,128,258]{1,2,0:T(8,128)} %get-tuple-element.36), channel_id=1, source_target_pairs={{0,2},{2,4},{4,6},{6,8},{8,10},{10,12},{12,14},{14,16},{16,18},{18... | collective-permute-start | bytes 396296 | tf_op jit(solution)/shard_map/ppermute | solution.py:16
  292.8 26.2 %collective-permute-start.10 = (f32[18,1,258]{2,0,1:T(8,128)}, f32[18,1,258]{2,0,1:T(8,128)}, u32[]{:S(2)}, u32[]{:S(2)}) collective-permute-start(f32[18,1,258]{2,0,1:T(8,128)} %copy.103), channel_id=1, source_target_pairs={{1,0},{3,2},{5,4},{7,6},{9,8},{11,10},{13,12},{15,14},{17,16},{19,... | collective-permute-start | bytes 55736 | tf_op jit(solution)/shard_map/ppermute | solution.py:19
  297.8 24.3 %collective-permute-start.11 = (f32[18,1,258]{2,0,1:T(8,128)}, f32[18,1,258]{2,0,1:T(8,128)}, u32[]{:S(2)}, u32[]{:S(2)}) collective-permute-start(f32[18,1,258]{2,0,1:T(8,128)} %copy.105), channel_id=1, source_target_pairs={{0,1},{2,3},{4,5},{6,7},{8,9},{10,11},{12,13},{14,15},{16,17},{18,... | collective-permute-start | bytes 55736 | tf_op jit(solution)/shard_map/ppermute | solution.py:16
  (20 other events, 404.9 us)
